TPU v7x, 128 devices: a whole 4x4x4 slice. The times are simulated.
128 devices in a mesh: ctx: 16 (over x, y_hi, core), head: 8 (over z, y_lo).
Axes of the slice: x: 4, y: 4 (y_hi: 2, y_lo: 2; y = y_hi * 2 + y_lo), z: 4, core: 2. Of those that a mesh axis runs over, the one named last changes fastest.
Arguments:
- hidden: bfloat16 [4096, 5120], P('ctx'), may hold values from -320 to 320
- positions: int32 [4096], replicated, may hold values from 0 to 4095, each once
- w_query: bfloat16 [5120, 5120], P(None, 'head'), may hold values from -0.078125 to 0.078125
- key_matrix: bfloat16 [5120, 1024], P(None, 'head'), may hold values from -0.15625 to 0.15625
- value_matrix: bfloat16 [5120, 1024], P(None, 'head'), may hold values from -0.078125 to 0.078125
- w_out: bfloat16 [5120, 5120], P('head'), may hold values from -0.3125 to 0.3125
- stored_keys: bfloat16 [24576, 1024], P('ctx', 'head'), may hold values from -33 to 33
- stored_values: bfloat16 [24576, 1024], P('ctx', 'head'), may hold values from -6 to 6
- kept_pages: int32 [8, 96], replicated, may hold values from 0 to 191, as said below
- page_slot: int32 [192], replicated, may hold values from 0 to 191, each once
Outputs:
- layer_out: float32 [4096, 5120], P('ctx', 'head')
Inputs may be any that keep to these rules, and one draw needn't show every extreme that they name: Each row of kept_pages names 96 different logical pages, page 0 and page 192 - 1 among them. `positions`: every position 0 to 4095 occurs once. `page_slot`: every slot occurs once; slot s holds cache rows s * 128 to s * 128 + 127.
All inputs are finite; a program needn't handle non-finite values.
Results may differ from a plain program's by a relative error of at most 0.0076.
Values may be sent and summed in bfloat16 or wider, within the bound.
A program may use at most 384 MiB of HBM per device.

v0:
```python
import math

import jax
import jax.numpy as jnp
from jax import lax
from jax.sharding import PartitionSpec as P

QUERY_GROUP = 5
HEAD_WIDTH = 128
PAGE = 128


masked_low = -1e30


def passed_along(value, axis, steps):
    count = lax.axis_size(axis)
    pairs = [(source, (source + steps) % count) for source in range(count)]
    return lax.ppermute(value, axis, pairs)


def temper(abs_pos, head_size):
    steps_num = ((abs_pos + 1) // 8192).astype(jnp.float32)
    return (jnp.log(steps_num + 1.0) * 0.1 + 1.0) / math.sqrt(head_size)


def keep_rows(kept_pages, page_slot, page_len):
    total_pages = page_slot.shape[0]
    page_numbers = jnp.arange(total_pages, dtype=jnp.int32)
    logical = jnp.any(kept_pages[:, :, None] == page_numbers[None, None, :], axis=1)
    onehot = page_slot[:, None] == page_numbers[None, :]
    physical = jnp.any(logical[:, :, None] & onehot[None], axis=1)
    return jnp.repeat(physical, page_len, axis=1)


def empty_state(kv_count, row_count):
    return (
        jnp.full((kv_count, QUERY_GROUP, row_count), masked_low, jnp.float32),
        jnp.zeros((kv_count, QUERY_GROUP, row_count), jnp.float32),
        jnp.zeros((kv_count, QUERY_GROUP, row_count, HEAD_WIDTH), jnp.float32),
    )


def absorb(carried, query_rows, key_rows, value_rows, allowed):
    maxima, totals, running = carried
    kv_count = query_rows.shape[1]
    keys_three = key_rows.reshape(key_rows.shape[0], kv_count, HEAD_WIDTH)
    values_three = value_rows.reshape(value_rows.shape[0], kv_count, HEAD_WIDTH)
    scores = jnp.einsum(
        "rkgd,skd->kgrs", query_rows, keys_three, preferred_element_type=jnp.float32
    )
    scores = jnp.where(allowed, scores, masked_low)
    new_max = jnp.maximum(maxima, jnp.max(scores, axis=-1))
    rescale = jnp.exp(maxima - new_max)
    weights = jnp.where(allowed, jnp.exp(scores - new_max[..., None]), 0.0)
    totals = totals * rescale + jnp.sum(weights, axis=-1)
    running = running * rescale[..., None] + jnp.einsum(
        "kgrs,skd->kgrd",
        weights.astype(jnp.bfloat16),
        values_three,
        preferred_element_type=jnp.float32,
    )
    return (new_max, totals, running)


def attend_cache(carried, query_rows, key_rows, value_rows, row_keep):
    return absorb(carried, query_rows, key_rows, value_rows, row_keep[:, None, None, :])


def on_device(
    hidden,
    positions,
    w_query,
    key_matrix,
    value_matrix,
    w_out,
    stored_keys,
    stored_values,
    kept_pages,
    page_slot,
):
    tokens = hidden.shape[0]
    kv_count = key_matrix.shape[1] // HEAD_WIDTH
    cycle_size = lax.axis_size("ctx")
    ctx_index = lax.axis_index("ctx")
    head_index = lax.axis_index("head")
    my_positions = lax.dynamic_slice_in_dim(positions, ctx_index * tokens, tokens, 0)
    cached_total = stored_keys.shape[0] * cycle_size
    scaling = temper(my_positions + cached_total, HEAD_WIDTH)
    query_rows = (
        jnp.dot(hidden, w_query, preferred_element_type=jnp.float32) * scaling[:, None]
    ).astype(jnp.bfloat16)
    query_rows = query_rows.reshape(tokens, kv_count, QUERY_GROUP, HEAD_WIDTH)
    turn_keys = jnp.dot(hidden, key_matrix, preferred_element_type=jnp.float32).astype(jnp.bfloat16)
    turn_values = jnp.dot(hidden, value_matrix, preferred_element_type=jnp.float32).astype(
        jnp.bfloat16
    )
    my_kept = lax.dynamic_slice_in_dim(kept_pages, head_index * kv_count, kv_count, 0)
    all_keep = keep_rows(my_kept, page_slot, PAGE)
    local_rows = stored_keys.shape[0]
    local_keep = lax.dynamic_slice_in_dim(all_keep, ctx_index * local_rows, local_rows, 1)
    key_piece = lax.all_gather(turn_keys, "ctx", axis=0, tiled=True)
    value_piece = lax.all_gather(turn_values, "ctx", axis=0, tiled=True)
    causal = positions[None, :] <= my_positions[:, None]
    carried = absorb(
        empty_state(kv_count, tokens), query_rows, key_piece, value_piece, causal[None, None]
    )

    def cycle_turn(turn_index, payload):
        visiting, running = payload
        running = attend_cache(running, visiting, stored_keys, stored_values, local_keep)
        visiting = passed_along(visiting, "ctx", 1)
        running = passed_along((running[0], running[1], running[2]), "ctx", 1)
        return (visiting, running)

    payload = lax.fori_loop(0, cycle_size, cycle_turn, (query_rows, carried))
    carried = payload[1]
    maxima, totals, running = carried
    head_outputs = (running / totals[..., None]).astype(jnp.bfloat16)
    out_weight = w_out.reshape(kv_count, QUERY_GROUP, HEAD_WIDTH, w_out.shape[1])
    partial_out = jnp.einsum(
        "kgrd,kgdn->rn", head_outputs, out_weight, preferred_element_type=jnp.float32
    )
    return lax.psum_scatter(partial_out, "head", scatter_dimension=1, tiled=True)


def solution(mesh):
    placed = (
        P("ctx", None),
        P(),
        P(None, "head"),
        P(None, "head"),
        P(None, "head"),
        P("head", None),
        P("ctx", "head"),
        P("ctx", "head"),
        P(),
        P(),
    )
    return jax.shard_map(
        on_device, mesh=mesh, in_specs=placed, out_specs=P("ctx", "head"), check_vma=False
    )
```

profile of v0, /device:TPU:0, one launch (start us, length us, event | category | flops | bytes accessed | tf_op | source)
XLA Modules:
  0.0 591.7 jit_solution(11534191287135701944)
XLA Ops:
  14.1 5.1 fusion.35
  23.4 35.2 %all-gather.3.cloned.1.call-done = bf16[4096,128]{1,0:T(8,128)(2,1)} async-done(((bf16[256,128]{1,0:T(8,128)(2,1)}), bf16[4096,128]{1,0:T(8,128)(2,1)}) %all-gather.3.cloned.1.call-update) | async-done | bytes 1048592 | tf_op jit(solution)/shard_map/all_gather | solution.py:102
  58.6 4.8 fusion.22
  70.4 34.4 %all-gather.5.cloned.1.call-done = bf16[4096,128]{1,0:T(8,128)(2,1)} async-done(((bf16[256,128]{1,0:T(8,128)(2,1)}), bf16[4096,128]{1,0:T(8,128)(2,1)}) %all-gather.5.cloned.1.call-update) | async-done | bytes 1048592 | tf_op jit(solution)/shard_map/all_gather | solution.py:103
  104.8 10.9 %fusion.32 = f32[1,5,256,128]{3,2,1,0:T(8,128)} fusion(f32[4096,256,5]{1,0,2:T(8,128)} %copy-done.1, f32[5,256]{1,0:T(8,128)S(1)} %get-tuple-element.98, pred[256,4096]{0,1:T(8,128)(4,1)} %broadcast_compare_fusion, bf16[4096,128]{1,0:T(8,128)(2,1)} %all-gather.5.cloned.1.call-done, f32[5,256]{1,0:T(8,128)S(1)} %get-tuple-element.96), kind=kOutput, calls=%fused_computation.35 | convolution fusion | flops 1363312640 | bytes 23734272 | tf_op jit(solution)/shard_map/kgrs,skd->kgrd/dot_general | solution.py:57
  115.7 352.0 %while.16 = (s32[]{:T(128)}, bf16[256,1,5,128]{3,0,2,1:T(8,128)(2,1)S(1)}, f32[1,5,256]{2,1,0:T(8,128)S(1)}, f32[1,5,256]{2,1,0:T(8,128)S(1)}, f32[1,5,256,128]{...) while((s32[]{:T(128)}, ...), condition=%wide.region_7.8_spmd, body=%wide.region_4.7_spmd.sunk | while | flops 1026625280 | bytes 32309024 | solution.py:116
  129.6 8.1 %collective-permute-done.2 = f32[1,5,256]{2,1,0:T(8,128)S(1)} collective-permute-done((f32[1,5,256]{2,1,0:T(8,128)S(1)}, f32[1,5,256]{2,1,0:T(8,128)S(1)}, u32[]{:S(2)}, u32[]{:S(2)}) %collective-permute-start.2) | collective-permute-done | bytes 5152 | tf_op jit(solution)/shard_map/while/body/eval_jaxpr/ppermute | solution.py:19
  150.3 10.4 %collective-permute-done.2 = f32[1,5,256]{2,1,0:T(8,128)S(1)} collective-permute-done((f32[1,5,256]{2,1,0:T(8,128)S(1)}, f32[1,5,256]{2,1,0:T(8,128)S(1)}, u32[]{:S(2)}, u32[]{:S(2)}) %collective-permute-start.2) | collective-permute-done | bytes 5152 | tf_op jit(solution)/shard_map/while/body/eval_jaxpr/ppermute | solution.py:19
  172.3 9.7 %collective-permute-done.2 = f32[1,5,256]{2,1,0:T(8,128)S(1)} collective-permute-done((f32[1,5,256]{2,1,0:T(8,128)S(1)}, f32[1,5,256]{2,1,0:T(8,128)S(1)}, u32[]{:S(2)}, u32[]{:S(2)}) %collective-permute-start.2) | collective-permute-done | bytes 5152 | tf_op jit(solution)/shard_map/while/body/eval_jaxpr/ppermute | solution.py:19
  193.1 10.3 %collective-permute-done.2 = f32[1,5,256]{2,1,0:T(8,128)S(1)} collective-permute-done((f32[1,5,256]{2,1,0:T(8,128)S(1)}, f32[1,5,256]{2,1,0:T(8,128)S(1)}, u32[]{:S(2)}, u32[]{:S(2)}) %collective-permute-start.2) | collective-permute-done | bytes 5152 | tf_op jit(solution)/shard_map/while/body/eval_jaxpr/ppermute | solution.py:19
  217.3 7.5 %collective-permute-done.2 = f32[1,5,256]{2,1,0:T(8,128)S(1)} collective-permute-done((f32[1,5,256]{2,1,0:T(8,128)S(1)}, f32[1,5,256]{2,1,0:T(8,128)S(1)}, u32[]{:S(2)}, u32[]{:S(2)}) %collective-permute-start.2) | collective-permute-done | bytes 5152 | tf_op jit(solution)/shard_map/while/body/eval_jaxpr/ppermute | solution.py:19
  238.0 10.4 %collective-permute-done.2 = f32[1,5,256]{2,1,0:T(8,128)S(1)} collective-permute-done((f32[1,5,256]{2,1,0:T(8,128)S(1)}, f32[1,5,256]{2,1,0:T(8,128)S(1)}, u32[]{:S(2)}, u32[]{:S(2)}) %collective-permute-start.2) | collective-permute-done | bytes 5152 | tf_op jit(solution)/shard_map/while/body/eval_jaxpr/ppermute | solution.py:19
  260.6 9.1 %collective-permute-done.2 = f32[1,5,256]{2,1,0:T(8,128)S(1)} collective-permute-done((f32[1,5,256]{2,1,0:T(8,128)S(1)}, f32[1,5,256]{2,1,0:T(8,128)S(1)}, u32[]{:S(2)}, u32[]{:S(2)}) %collective-permute-start.2) | collective-permute-done | bytes 5152 | tf_op jit(solution)/shard_map/while/body/eval_jaxpr/ppermute | solution.py:19
  282.6 9.1 %collective-permute-done.2 = f32[1,5,256]{2,1,0:T(8,128)S(1)} collective-permute-done((f32[1,5,256]{2,1,0:T(8,128)S(1)}, f32[1,5,256]{2,1,0:T(8,128)S(1)}, u32[]{:S(2)}, u32[]{:S(2)}) %collective-permute-start.2) | collective-permute-done | bytes 5152 | tf_op jit(solution)/shard_map/while/body/eval_jaxpr/ppermute | solution.py:19
  305.6 8.1 %collective-permute-done.2 = f32[1,5,256]{2,1,0:T(8,128)S(1)} collective-permute-done((f32[1,5,256]{2,1,0:T(8,128)S(1)}, f32[1,5,256]{2,1,0:T(8,128)S(1)}, u32[]{:S(2)}, u32[]{:S(2)}) %collective-permute-start.2) | collective-permute-done | bytes 5152 | tf_op jit(solution)/shard_map/while/body/eval_jaxpr/ppermute | solution.py:19
  327.0 9.7 %collective-permute-done.2 = f32[1,5,256]{2,1,0:T(8,128)S(1)} collective-permute-done((f32[1,5,256]{2,1,0:T(8,128)S(1)}, f32[1,5,256]{2,1,0:T(8,128)S(1)}, u32[]{:S(2)}, u32[]{:S(2)}) %collective-permute-start.2) | collective-permute-done | bytes 5152 | tf_op jit(solution)/shard_map/while/body/eval_jaxpr/ppermute | solution.py:19
  348.3 9.7 %collective-permute-done.2 = f32[1,5,256]{2,1,0:T(8,128)S(1)} collective-permute-done((f32[1,5,256]{2,1,0:T(8,128)S(1)}, f32[1,5,256]{2,1,0:T(8,128)S(1)}, u32[]{:S(2)}, u32[]{:S(2)}) %collective-permute-start.2) | collective-permute-done | bytes 5152 | tf_op jit(solution)/shard_map/while/body/eval_jaxpr/ppermute | solution.py:19
  369.7 9.7 %collective-permute-done.2 = f32[1,5,256]{2,1,0:T(8,128)S(1)} collective-permute-done((f32[1,5,256]{2,1,0:T(8,128)S(1)}, f32[1,5,256]{2,1,0:T(8,128)S(1)}, u32[]{:S(2)}, u32[]{:S(2)}) %collective-permute-start.2) | collective-permute-done | bytes 5152 | tf_op jit(solution)/shard_map/while/body/eval_jaxpr/ppermute | solution.py:19
  393.3 7.5 %collective-permute-done.2 = f32[1,5,256]{2,1,0:T(8,128)S(1)} collective-permute-done((f32[1,5,256]{2,1,0:T(8,128)S(1)}, f32[1,5,256]{2,1,0:T(8,128)S(1)}, u32[]{:S(2)}, u32[]{:S(2)}) %collective-permute-start.2) | collective-permute-done | bytes 5152 | tf_op jit(solution)/shard_map/while/body/eval_jaxpr/ppermute | solution.py:19
  414.7 9.7 %collective-permute-done.2 = f32[1,5,256]{2,1,0:T(8,128)S(1)} collective-permute-done((f32[1,5,256]{2,1,0:T(8,128)S(1)}, f32[1,5,256]{2,1,0:T(8,128)S(1)}, u32[]{:S(2)}, u32[]{:S(2)}) %collective-permute-start.2) | collective-permute-done | bytes 5152 | tf_op jit(solution)/shard_map/while/body/eval_jaxpr/ppermute | solution.py:19
  436.6 9.1 %collective-permute-done.2 = f32[1,5,256]{2,1,0:T(8,128)S(1)} collective-permute-done((f32[1,5,256]{2,1,0:T(8,128)S(1)}, f32[1,5,256]{2,1,0:T(8,128)S(1)}, u32[]{:S(2)}, u32[]{:S(2)}) %collective-permute-start.2) | collective-permute-done | bytes 5152 | tf_op jit(solution)/shard_map/while/body/eval_jaxpr/ppermute | solution.py:19
  458.6 9.1 %collective-permute-done.2 = f32[1,5,256]{2,1,0:T(8,128)S(1)} collective-permute-done((f32[1,5,256]{2,1,0:T(8,128)S(1)}, f32[1,5,256]{2,1,0:T(8,128)S(1)}, u32[]{:S(2)}, u32[]{:S(2)}) %collective-permute-start.2) | collective-permute-done | bytes 5152 | tf_op jit(solution)/shard_map/while/body/eval_jaxpr/ppermute | solution.py:19
  467.7 7.7 %convolution_bitcast_fusion = f32[256,5120]{1,0:T(8,128)} fusion(bf16[5,128,5120]{2,1,0:T(8,128)(2,1)} %bitcast.157, f32[1,5,256,128]{3,2,1,0:T(8,128)} %get-tuple-element.48, f32[5,256]{1,0:T(8,128)S(1)} %bitcast.162), kind=kOutput, calls=%fused_computation.31 | convolution fusion | flops 1678049280 | bytes 12456960 | tf_op jit(solution)/shard_map/kgrd,kgdn->rn/dot_general | solution.py:121
  475.3 109.9 %reduce-scatter.2.cloned.1.call-done = f32[256,640]{1,0:T(8,128)} async-done(((f32[256,5120]{1,0:T(8,128)}), f32[256,640]{1,0:T(8,128)}) %reduce-scatter.2.cloned.1.call-update) | async-done | bytes 655376 | tf_op jit(solution)/shard_map/reduce_scatter | solution.py:124
  (303 shorter events, 222.5 us)
Async XLA Ops:
  6.5 52.1 %all-gather.3.cloned.1.call-start = ((), (), s32[]{:S(2)}) async-start(), calls=%async_computation.1 | async-start | bytes 1114112 | tf_op jit(solution)/shard_map/all_gather | solution.py:102
  11.1 93.7 %all-gather.5.cloned.1.call-start = ((), (), s32[]{:S(2)}) async-start(), calls=%async_computation.2 | async-start | bytes 1114112 | tf_op jit(solution)/shard_map/all_gather | solution.py:103
  13.9 571.3 %reduce-scatter.2.cloned.1.call-start = ((), (), s32[]{:S(2)}) async-start(), calls=%async_computation.3 | async-start | bytes 5898240 | tf_op jit(solution)/shard_map/reduce_scatter | solution.py:124
  115.7 21.9 %collective-permute-start = (bf16[256,1,5,128]{3,0,2,1:T(8,128)(2,1)S(1)}, bf16[256,1,5,128]{3,0,2,1:T(8,128)(2,1)S(1)}, u32[]{:S(2)}, u32[]{:S(2)}) collective-permute-start(bf16[256,1,5,128]{3,0,2,1:T(8,128)(2,1)S(1)} %copy.36), channel_id=1, source_target_pairs={{0,8},{8,16},{16,24},{24,32},{32,40},{40,48},{48,56},{56,64},{64,7... | collective-permute-start | bytes 983048 | tf_op jit(solution)/shard_map/while/body/eval_jaxpr/ppermute | solution.py:19
  123.7 13.9 %collective-permute-start.3 = (f32[1,5,256,128]{3,2,1,0:T(8,128)}, f32[1,5,256,128]{3,2,1,0:T(8,128)}, u32[]{:S(2)}, u32[]{:S(2)}) collective-permute-start(f32[1,5,256,128]{3,2,1,0:T(8,128)} %fusion.63), channel_id=1, source_target_pairs={{0,8},{8,16},{16,24},{24,32},{32,40},{40,48},{48,56},{56,64},{64,7... | collective-permute-start | bytes 1966088 | tf_op jit(solution)/shard_map/while/body/eval_jaxpr/ppermute | solution.py:19
  137.7 23.0 %collective-permute-start = (bf16[256,1,5,128]{3,0,2,1:T(8,128)(2,1)S(1)}, bf16[256,1,5,128]{3,0,2,1:T(8,128)(2,1)S(1)}, u32[]{:S(2)}, u32[]{:S(2)}) collective-permute-start(bf16[256,1,5,128]{3,0,2,1:T(8,128)(2,1)S(1)} %copy.36), channel_id=1, source_target_pairs={{0,8},{8,16},{16,24},{24,32},{32,40},{40,48},{48,56},{56,64},{64,7... | collective-permute-start | bytes 983048 | tf_op jit(solution)/shard_map/while/body/eval_jaxpr/ppermute | solution.py:19
  146.8 13.9 %collective-permute-start.3 = (f32[1,5,256,128]{3,2,1,0:T(8,128)}, f32[1,5,256,128]{3,2,1,0:T(8,128)}, u32[]{:S(2)}, u32[]{:S(2)}) collective-permute-start(f32[1,5,256,128]{3,2,1,0:T(8,128)} %fusion.63), channel_id=1, source_target_pairs={{0,8},{8,16},{16,24},{24,32},{32,40},{40,48},{48,56},{56,64},{64,7... | collective-permute-start | bytes 1966088 | tf_op jit(solution)/shard_map/while/body/eval_jaxpr/ppermute | solution.py:19
  160.7 21.3 %collective-permute-start = (bf16[256,1,5,128]{3,0,2,1:T(8,128)(2,1)S(1)}, bf16[256,1,5,128]{3,0,2,1:T(8,128)(2,1)S(1)}, u32[]{:S(2)}, u32[]{:S(2)}) collective-permute-start(bf16[256,1,5,128]{3,0,2,1:T(8,128)(2,1)S(1)} %copy.36), channel_id=1, source_target_pairs={{0,8},{8,16},{16,24},{24,32},{32,40},{40,48},{48,56},{56,64},{64,7... | collective-permute-start | bytes 983048 | tf_op jit(solution)/shard_map/while/body/eval_jaxpr/ppermute | solution.py:19
  168.1 13.9 %collective-permute-start.3 = (f32[1,5,256,128]{3,2,1,0:T(8,128)}, f32[1,5,256,128]{3,2,1,0:T(8,128)}, u32[]{:S(2)}, u32[]{:S(2)}) collective-permute-start(f32[1,5,256,128]{3,2,1,0:T(8,128)} %fusion.63), channel_id=1, source_target_pairs={{0,8},{8,16},{16,24},{24,32},{32,40},{40,48},{48,56},{56,64},{64,7... | collective-permute-start | bytes 1966088 | tf_op jit(solution)/shard_map/while/body/eval_jaxpr/ppermute | solution.py:19
  182.1 21.3 %collective-permute-start = (bf16[256,1,5,128]{3,0,2,1:T(8,128)(2,1)S(1)}, bf16[256,1,5,128]{3,0,2,1:T(8,128)(2,1)S(1)}, u32[]{:S(2)}, u32[]{:S(2)}) collective-permute-start(bf16[256,1,5,128]{3,0,2,1:T(8,128)(2,1)S(1)} %copy.36), channel_id=1, source_target_pairs={{0,8},{8,16},{16,24},{24,32},{32,40},{40,48},{48,56},{56,64},{64,7... | collective-permute-start | bytes 983048 | tf_op jit(solution)/shard_map/while/body/eval_jaxpr/ppermute | solution.py:19
  189.5 13.9 %collective-permute-start.3 = (f32[1,5,256,128]{3,2,1,0:T(8,128)}, f32[1,5,256,128]{3,2,1,0:T(8,128)}, u32[]{:S(2)}, u32[]{:S(2)}) collective-permute-start(f32[1,5,256,128]{3,2,1,0:T(8,128)} %fusion.63), channel_id=1, source_target_pairs={{0,8},{8,16},{16,24},{24,32},{32,40},{40,48},{48,56},{56,64},{64,7... | collective-permute-start | bytes 1966088 | tf_op jit(solution)/shard_map/while/body/eval_jaxpr/ppermute | solution.py:19
  203.5 21.3 %collective-permute-start = (bf16[256,1,5,128]{3,0,2,1:T(8,128)(2,1)S(1)}, bf16[256,1,5,128]{3,0,2,1:T(8,128)(2,1)S(1)}, u32[]{:S(2)}, u32[]{:S(2)}) collective-permute-start(bf16[256,1,5,128]{3,0,2,1:T(8,128)(2,1)S(1)} %copy.36), channel_id=1, source_target_pairs={{0,8},{8,16},{16,24},{24,32},{32,40},{40,48},{48,56},{56,64},{64,7... | collective-permute-start | bytes 983048 | tf_op jit(solution)/shard_map/while/body/eval_jaxpr/ppermute | solution.py:19
  210.9 13.9 %collective-permute-start.3 = (f32[1,5,256,128]{3,2,1,0:T(8,128)}, f32[1,5,256,128]{3,2,1,0:T(8,128)}, u32[]{:S(2)}, u32[]{:S(2)}) collective-permute-start(f32[1,5,256,128]{3,2,1,0:T(8,128)} %fusion.63), channel_id=1, source_target_pairs={{0,8},{8,16},{16,24},{24,32},{32,40},{40,48},{48,56},{56,64},{64,7... | collective-permute-start | bytes 1966088 | tf_op jit(solution)/shard_map/while/body/eval_jaxpr/ppermute | solution.py:19
  224.8 23.5 %collective-permute-start = (bf16[256,1,5,128]{3,0,2,1:T(8,128)(2,1)S(1)}, bf16[256,1,5,128]{3,0,2,1:T(8,128)(2,1)S(1)}, u32[]{:S(2)}, u32[]{:S(2)}) collective-permute-start(bf16[256,1,5,128]{3,0,2,1:T(8,128)(2,1)S(1)} %copy.36), channel_id=1, source_target_pairs={{0,8},{8,16},{16,24},{24,32},{32,40},{40,48},{48,56},{56,64},{64,7... | collective-permute-start | bytes 983048 | tf_op jit(solution)/shard_map/while/body/eval_jaxpr/ppermute | solution.py:19
  248.4 21.3 %collective-permute-start = (bf16[256,1,5,128]{3,0,2,1:T(8,128)(2,1)S(1)}, bf16[256,1,5,128]{3,0,2,1:T(8,128)(2,1)S(1)}, u32[]{:S(2)}, u32[]{:S(2)}) collective-permute-start(bf16[256,1,5,128]{3,0,2,1:T(8,128)(2,1)S(1)} %copy.36), channel_id=1, source_target_pairs={{0,8},{8,16},{16,24},{24,32},{32,40},{40,48},{48,56},{56,64},{64,7... | collective-permute-start | bytes 983048 | tf_op jit(solution)/shard_map/while/body/eval_jaxpr/ppermute | solution.py:19
  269.8 21.9 %collective-permute-start = (bf16[256,1,5,128]{3,0,2,1:T(8,128)(2,1)S(1)}, bf16[256,1,5,128]{3,0,2,1:T(8,128)(2,1)S(1)}, u32[]{:S(2)}, u32[]{:S(2)}) collective-permute-start(bf16[256,1,5,128]{3,0,2,1:T(8,128)(2,1)S(1)} %copy.36), channel_id=1, source_target_pairs={{0,8},{8,16},{16,24},{24,32},{32,40},{40,48},{48,56},{56,64},{64,7... | collective-permute-start | bytes 983048 | tf_op jit(solution)/shard_map/while/body/eval_jaxpr/ppermute | solution.py:19
  291.7 22.0 %collective-permute-start = (bf16[256,1,5,128]{3,0,2,1:T(8,128)(2,1)S(1)}, bf16[256,1,5,128]{3,0,2,1:T(8,128)(2,1)S(1)}, u32[]{:S(2)}, u32[]{:S(2)}) collective-permute-start(bf16[256,1,5,128]{3,0,2,1:T(8,128)(2,1)S(1)} %copy.36), channel_id=1, source_target_pairs={{0,8},{8,16},{16,24},{24,32},{32,40},{40,48},{48,56},{56,64},{64,7... | collective-permute-start | bytes 983048 | tf_op jit(solution)/shard_map/while/body/eval_jaxpr/ppermute | solution.py:19
  313.7 23.0 %collective-permute-start = (bf16[256,1,5,128]{3,0,2,1:T(8,128)(2,1)S(1)}, bf16[256,1,5,128]{3,0,2,1:T(8,128)(2,1)S(1)}, u32[]{:S(2)}, u32[]{:S(2)}) collective-permute-start(bf16[256,1,5,128]{3,0,2,1:T(8,128)(2,1)S(1)} %copy.36), channel_id=1, source_target_pairs={{0,8},{8,16},{16,24},{24,32},{32,40},{40,48},{48,56},{56,64},{64,7... | collective-permute-start | bytes 983048 | tf_op jit(solution)/shard_map/while/body/eval_jaxpr/ppermute | solution.py:19
  336.7 21.3 %collective-permute-start = (bf16[256,1,5,128]{3,0,2,1:T(8,128)(2,1)S(1)}, bf16[256,1,5,128]{3,0,2,1:T(8,128)(2,1)S(1)}, u32[]{:S(2)}, u32[]{:S(2)}) collective-permute-start(bf16[256,1,5,128]{3,0,2,1:T(8,128)(2,1)S(1)} %copy.36), channel_id=1, source_target_pairs={{0,8},{8,16},{16,24},{24,32},{32,40},{40,48},{48,56},{56,64},{64,7... | collective-permute-start | bytes 983048 | tf_op jit(solution)/shard_map/while/body/eval_jaxpr/ppermute | solution.py:19
  358.1 21.3 %collective-permute-start = (bf16[256,1,5,128]{3,0,2,1:T(8,128)(2,1)S(1)}, bf16[256,1,5,128]{3,0,2,1:T(8,128)(2,1)S(1)}, u32[]{:S(2)}, u32[]{:S(2)}) collective-permute-start(bf16[256,1,5,128]{3,0,2,1:T(8,128)(2,1)S(1)} %copy.36), channel_id=1, source_target_pairs={{0,8},{8,16},{16,24},{24,32},{32,40},{40,48},{48,56},{56,64},{64,7... | collective-permute-start | bytes 983048 | tf_op jit(solution)/shard_map/while/body/eval_jaxpr/ppermute | solution.py:19
  379.5 21.3 %collective-permute-start = (bf16[256,1,5,128]{3,0,2,1:T(8,128)(2,1)S(1)}, bf16[256,1,5,128]{3,0,2,1:T(8,128)(2,1)S(1)}, u32[]{:S(2)}, u32[]{:S(2)}) collective-permute-start(bf16[256,1,5,128]{3,0,2,1:T(8,128)(2,1)S(1)} %copy.36), channel_id=1, source_target_pairs={{0,8},{8,16},{16,24},{24,32},{32,40},{40,48},{48,56},{56,64},{64,7... | collective-permute-start | bytes 983048 | tf_op jit(solution)/shard_map/while/body/eval_jaxpr/ppermute | solution.py:19
  400.8 23.5 %collective-permute-start = (bf16[256,1,5,128]{3,0,2,1:T(8,128)(2,1)S(1)}, bf16[256,1,5,128]{3,0,2,1:T(8,128)(2,1)S(1)}, u32[]{:S(2)}, u32[]{:S(2)}) collective-permute-start(bf16[256,1,5,128]{3,0,2,1:T(8,128)(2,1)S(1)} %copy.36), channel_id=1, source_target_pairs={{0,8},{8,16},{16,24},{24,32},{32,40},{40,48},{48,56},{56,64},{64,7... | collective-permute-start | bytes 983048 | tf_op jit(solution)/shard_map/while/body/eval_jaxpr/ppermute | solution.py:19
  424.4 21.3 %collective-permute-start = (bf16[256,1,5,128]{3,0,2,1:T(8,128)(2,1)S(1)}, bf16[256,1,5,128]{3,0,2,1:T(8,128)(2,1)S(1)}, u32[]{:S(2)}, u32[]{:S(2)}) collective-permute-start(bf16[256,1,5,128]{3,0,2,1:T(8,128)(2,1)S(1)} %copy.36), channel_id=1, source_target_pairs={{0,8},{8,16},{16,24},{24,32},{32,40},{40,48},{48,56},{56,64},{64,7... | collective-permute-start | bytes 983048 | tf_op jit(solution)/shard_map/while/body/eval_jaxpr/ppermute | solution.py:19
  445.8 21.9 %collective-permute-start = (bf16[256,1,5,128]{3,0,2,1:T(8,128)(2,1)S(1)}, bf16[256,1,5,128]{3,0,2,1:T(8,128)(2,1)S(1)}, u32[]{:S(2)}, u32[]{:S(2)}) collective-permute-start(bf16[256,1,5,128]{3,0,2,1:T(8,128)(2,1)S(1)} %copy.36), channel_id=1, source_target_pairs={{0,8},{8,16},{16,24},{24,32},{32,40},{40,48},{48,56},{56,64},{64,7... | collective-permute-start | bytes 983048 | tf_op jit(solution)/shard_map/while/body/eval_jaxpr/ppermute | solution.py:19
  (64 other events, 587.0 us)
Sparse Core Ops, SparseCore 0:
  11.2 47.3 all-gather.2
  61.0 43.7 all-gather.4
  475.5 109.6 reduce-scatter.1
where the time goes:
time: 594 us; the launch traced here: 592 us
  waiting for transfers between devices  327 us (55%)
  matrix products  148 us (25%)
  starting transfers between devices  56.3 us (9%)
  other arithmetic  40.2 us (7%)
  between operations  13.2 us (2%)
    ppermute x64, waiting for transfers between devices, passed_along(): return lax.ppermute(value, axis, pairs)  147 us
    reduce_scatter x1, waiting for transfers between devices, on_device(): lax.psum_scatter(partial_out, 'head', scatter_dimension=1, tiled=True)  110 us
    dot_general x17, matrix products, absorb(): jnp.einsum('kgrs,skd->kgrd', weights.astype(jnp.bfloat16), values_three,...  82.8 us
    ppermute x64, starting transfers between devices, passed_along(): return lax.ppermute(value, axis, pairs)  56.2 us
    dot_general x17, matrix products, absorb(): jnp.einsum('rkgd,skd->kgrs', query_rows, keys_three, preferred_element_ty...  47.3 us
    reduce_sum x17, other arithmetic, absorb(): totals = totals * rescale + jnp.sum(weights, axis=-1)  36.4 us
    all_gather x1, waiting for transfers between devices, on_device(): key_piece = lax.all_gather(turn_keys, 'ctx', axis=0, tiled=True)  35.2 us
    all_gather x1, waiting for transfers between devices, on_device(): value_piece = lax.all_gather(turn_values, 'ctx', axis=0, tiled=True)  34.4 us
  transfers between devices with their start and end apart: 67, of which 19 were waited for; matrix products, arithmetic and copies ran while one was open for 28% of the time, Pallas kernels for 0%

commit v1 on v0

v1 whole, which is shorter than its diff:
```python
import functools
import math

import jax
import jax.numpy as jnp
from jax import lax
from jax.experimental import pallas as pl
from jax.experimental.pallas import tpu as pltpu
from jax.sharding import PartitionSpec as P

G = 5
W = 128
PAGE = 128
LOW = -1e30
MASKED = -3e38
MESH = pl.DeviceIdType.MESH
F32 = jnp.float32
BF16 = jnp.bfloat16


def places(x_count):
    ctx = lax.axis_index("ctx")
    head = lax.axis_index("head")
    x, y_hi, core = ctx // 4, (ctx // 2) % 2, ctx % 2

    def at(dx=0, dy=0, dc=0):
        return (lax.rem(x + dx, x_count) * 2 + lax.rem(y_hi + dy, 2)) * 2 + lax.rem(core + dc, 2)

    return ctx, head, core, at


def gather_kernel(
    x_count,
    z_count,
    scale_base,
    positions_ref,
    hidden_ref,
    w_query_ref,
    w_key_ref,
    w_value_ref,
    w_out_ref,
    keys_ref,
    values_ref,
    all_keys,
    all_values,
    all_new,
    queries,
    w_slab,
    hidden_vmem,
    wq_vmem,
    wk_vmem,
    wv_vmem,
    acc_vmem,
    q_vmem,
    new_vmem,
    send_sem,
    recv_sem,
    load_sem,
    local_sem,
):
    ctx, head, core, at = places(x_count)
    z, y_lo = head // 2, head % 2
    tokens = hidden_ref.shape[0]
    half = w_out_ref.shape[0] // 2
    columns = w_slab.shape[2]
    depth = hidden_ref.shape[1]
    steps = load_sem.shape[0]
    cut = depth // steps

    right, left, far = at(dx=1), at(dx=x_count - 1), at(dx=2)
    sibling, y_peer = at(dc=1), at(dy=1)
    cross = (ctx // 4 * 2 + lax.rem((ctx // 2) % 2 + core, 2)) * 2 + core
    out_peers = []
    for dz in range(z_count):
        for dl in range(2):
            if dz or dl:
                other = lax.rem(z + dz, z_count) * 2 + lax.rem(y_lo + dl, 2)
                back = lax.rem(z + z_count - dz, z_count) * 2 + lax.rem(y_lo + dl, 2)
                out_peers.append((cross if dl else ctx, other, back))

    barrier = pltpu.get_barrier_semaphore()
    met = [(c, head) for c in (right, left, far, sibling, y_peer)]
    met += [(c, h) for c, h, _ in out_peers]
    for device in met:
        pl.semaphore_signal(barrier, inc=1, device_id=device, device_id_type=MESH)
    pl.semaphore_wait(barrier, len(met))

    counter = [0]

    def send(source, target, device):
        i = counter[0]
        counter[0] += 1
        copy = pltpu.make_async_remote_copy(
            src_ref=source,
            dst_ref=target,
            send_sem=send_sem.at[i],
            recv_sem=recv_sem.at[i],
            device_id=device,
            device_id_type=MESH,
        )
        copy.start()
        return copy

    near = []
    for mine, everyone in ((keys_ref, all_keys), (values_ref, all_values)):
        near.append(send(mine, everyone.at[2 * (x_count - 1)], (right, head)))
        near.append(send(mine, everyone.at[2], (left, head)))
    pair = [
        send(mine, everyone.at[1], (sibling, head))
        for mine, everyone in ((keys_ref, all_keys), (values_ref, all_values))
    ]
    loads = []
    for i in range(steps):
        rows = pl.ds(i * cut, cut)
        pieces = [
            pltpu.make_async_copy(hidden_ref.at[:, rows], hidden_vmem.at[:, rows], load_sem.at[i, 0]),
            pltpu.make_async_copy(w_query_ref.at[rows], wq_vmem.at[rows], load_sem.at[i, 1]),
            pltpu.make_async_copy(w_key_ref.at[rows], wk_vmem.at[rows], load_sem.at[i, 2]),
            pltpu.make_async_copy(w_value_ref.at[rows], wv_vmem.at[rows], load_sem.at[i, 3]),
        ]
        for piece in pieces:
            piece.start()
        loads.append(pieces)
    my_half = pl.ds(pl.multiple_of(core * half, half), half)
    slabs = []
    for c, h, back in out_peers:
        cols = pl.ds(pl.multiple_of(h * columns, columns), columns)
        copy = send(w_out_ref.at[my_half, cols], w_slab.at[head, my_half], (c, h))
        slabs.append((copy, back))
    my_cols = pl.ds(pl.multiple_of(head * columns, columns), columns)
    own = [
        pltpu.make_async_copy(keys_ref, all_keys.at[0], local_sem.at[0]),
        pltpu.make_async_copy(values_ref, all_values.at[0], local_sem.at[1]),
        pltpu.make_async_copy(w_out_ref.at[:, my_cols], w_slab.at[head], local_sem.at[2]),
    ]
    for copy in own:
        copy.start()

    q_cols = wq_vmem.shape[1]
    for i in range(steps):
        for piece in loads[i]:
            piece.wait()
        rows = slice(i * cut, (i + 1) * cut)
        part = hidden_vmem[:, rows]
        for w_ref, first, last in (
            (wq_vmem, 0, q_cols),
            (wk_vmem, q_cols, q_cols + W),
            (wv_vmem, q_cols + W, q_cols + 2 * W),
        ):
            product = jnp.dot(part, w_ref[rows, :], preferred_element_type=F32)
            if i:
                acc_vmem[:, first:last] += product
            else:
                acc_vmem[:, first:last] = product
    my_positions = positions_ref[pl.ds(ctx, 1), :]
    spread = jnp.broadcast_to(my_positions, (tokens, tokens))
    diagonal = lax.broadcasted_iota(jnp.int32, (tokens, tokens), 0) == lax.broadcasted_iota(
        jnp.int32, (tokens, tokens), 1
    )
    column = jnp.sum(jnp.where(diagonal, spread, 0).astype(F32), axis=1, keepdims=True)
    thousands = jnp.floor((column + (scale_base + 1.0)) * (1.0 / 8192.0))
    scaling = (jnp.log(thousands + 1.0) * 0.1 + 1.0) / math.sqrt(W)
    q_vmem[...] = (acc_vmem[:, :q_cols] * scaling).astype(BF16)
    new_vmem[...] = acc_vmem[:, q_cols:].astype(BF16)

    rows_own, rows_peer = pl.ds(0, tokens), pl.ds(tokens, tokens)
    ask = send(q_vmem, queries.at[rows_peer], (y_peer, head))
    fresh = [
        send(new_vmem, all_new.at[2 * (x_count - 1)], (right, head)),
        send(new_vmem, all_new.at[2], (left, head)),
        send(new_vmem, all_new.at[4], (far, head)),
    ]
    fresh_pair = [send(new_vmem, all_new.at[1], (sibling, head))]
    late = [
        pltpu.make_async_copy(q_vmem, queries.at[rows_own], local_sem.at[3]),
        pltpu.make_async_copy(new_vmem, all_new.at[0], local_sem.at[4]),
    ]
    for copy in late:
        copy.start()
    for copy, slot in zip(fresh, (2 * (x_count - 1), 2, 4)):
        copy.wait_recv()
        fresh_pair.append(send(all_new.at[slot], all_new.at[slot + 1], (sibling, head)))

    last = 2 * (x_count - 1)
    across = []
    for copy, everyone, slot in zip(
        near, (all_keys, all_keys, all_values, all_values), (last, 2, last, 2)
    ):
        copy.wait_recv()
        if everyone is all_keys and slot == last:
            across.append(send(all_keys.at[last], all_keys.at[4], (right, head)))
        if everyone is all_values and slot == 2:
            across.append(send(all_values.at[2], all_values.at[4], (left, head)))
        pair.append(send(everyone.at[slot], everyone.at[slot + 1], (sibling, head)))
    slab_pair = []
    for copy, back in slabs:
        copy.wait_recv()
        slab_pair.append(send(w_slab.at[back, my_half], w_slab.at[back, my_half], (sibling, head)))
    for copy, everyone in zip(across, (all_keys, all_values)):
        copy.wait_recv()
        pair.append(send(everyone.at[4], everyone.at[5], (sibling, head)))
    for copy in pair + fresh_pair + slab_pair + [ask]:
        copy.wait_recv()
    for copy in near + pair + fresh + fresh_pair + across + slab_pair + [ask]:
        copy.wait_send()
    for copy, _ in slabs:
        copy.wait_send()
    for copy in own + late:
        copy.wait()


def gather(positions, hidden, w_query, w_key, w_value, w_out, keys, values, x_count, z_count):
    rows = keys.shape[0]
    tokens, depth = hidden.shape
    q_cols = w_query.shape[1]
    columns = w_out.shape[1] // (2 * z_count)
    anywhere = pl.BlockSpec(memory_space=pl.ANY)
    steps = 5
    copies = 40
    return pl.pallas_call(
        functools.partial(gather_kernel, x_count, z_count, float(rows * x_count * 4)),
        out_shape=[
            jax.ShapeDtypeStruct((2 * x_count, rows, W), BF16),
            jax.ShapeDtypeStruct((2 * x_count, rows, W), BF16),
            jax.ShapeDtypeStruct((2 * x_count, tokens, 2 * W), BF16),
            jax.ShapeDtypeStruct((2 * tokens, q_cols), BF16),
            jax.ShapeDtypeStruct((2 * z_count, w_out.shape[0], columns), BF16),
        ],
        in_specs=[pl.BlockSpec(memory_space=pltpu.VMEM)] + [anywhere] * 7,
        out_specs=[anywhere] * 5,
        scratch_shapes=[
            pltpu.VMEM((tokens, depth), BF16),
            pltpu.VMEM((depth, q_cols), BF16),
            pltpu.VMEM((depth, W), BF16),
            pltpu.VMEM((depth, W), BF16),
            pltpu.VMEM((tokens, q_cols + 2 * W), F32),
            pltpu.VMEM((tokens, q_cols), BF16),
            pltpu.VMEM((tokens, 2 * W), BF16),
            pltpu.SemaphoreType.DMA((copies,)),
            pltpu.SemaphoreType.DMA((copies,)),
            pltpu.SemaphoreType.DMA((steps, 4)),
            pltpu.SemaphoreType.DMA((5,)),
        ],
        compiler_params=pltpu.CompilerParams(
            collective_id=0, has_side_effects=True, vmem_limit_bytes=40 * 2**20
        ),
    )(positions, hidden, w_query, w_key, w_value, w_out, keys, values)


def attend_kernel(
    x_count,
    kept_ref,
    slot_ref,
    place_ref,
    positions_ref,
    q_ref,
    k_ref,
    v_ref,
    new_ref,
    acc_ref,
    stats_ref,
    m_ref,
    l_ref,
    bias_ref,
    list_ref,
):
    ctx, head = place_ref[0], place_ref[1]
    x, y_hi, core = ctx // 4, (ctx // 2) % 2, ctx % 2
    kept_count = kept_ref.shape[1]
    per_device = slot_ref.shape[0] // (4 * x_count)
    rows = q_ref.shape[0]
    tokens = rows // 2
    step = 4

    def note(i, count):
        slot = slot_ref[kept_ref[head, i]]
        where = slot // per_device
        place = lax.rem(where // 4 - x + x_count, x_count) * 2 + lax.rem(where % 2 + core, 2)
        list_ref[count] = place * per_device + slot % per_device
        return count + jnp.where((where // 2) % 2 == y_hi, 1, 0)

    count = lax.fori_loop(0, kept_count, note, jnp.int32(0))
    for j in range(step):
        list_ref[count + j] = 0

    m_ref[...] = jnp.full_like(m_ref, LOW)
    l_ref[...] = jnp.zeros_like(l_ref)
    acc_ref[...] = jnp.zeros_like(acc_ref)

    def absorb(keys, values, bias):
        width = keys.shape[0] // W
        values = jnp.concatenate([values, jnp.ones_like(values)], axis=1)
        for g in range(G):
            q = q_ref[:, g * W : (g + 1) * W]
            s = lax.dot_general(q, keys, (((1,), (1,)), ((), ())), preferred_element_type=F32)
            if bias is not None:
                s = s + bias()
            m_old = m_ref[g]
            m_new = jnp.maximum(m_old, jnp.max(s, axis=1, keepdims=True))
            rescale = jnp.exp(m_old - m_new)
            p = jnp.exp(s - jnp.concatenate([m_new] * width, axis=1)).astype(BF16)
            summed = jnp.dot(p, values, preferred_element_type=F32)
            l_ref[g] = l_ref[g] * rescale + summed[:, W:]
            acc_ref[g] = acc_ref[g] * rescale + summed[:, :W]
            m_ref[g] = m_new

    def pages(first):
        ks, vs = [], []
        for j in range(step):
            here = pl.ds(pl.multiple_of(list_ref[first + j] * PAGE, PAGE), PAGE)
            ks.append(k_ref[here, :])
            vs.append(v_ref[here, :])
        return jnp.concatenate(ks, axis=0), jnp.concatenate(vs, axis=0)

    def full(i, _):
        keys, values = pages(i * step)
        absorb(keys, values, None)
        return 0

    lax.fori_loop(0, count // step, full, 0)

    @pl.when(count % step > 0)
    def _():
        first = count // step * step
        keys, values = pages(first)
        lane = lax.broadcasted_iota(jnp.int32, (1, step * PAGE), 1) // PAGE
        row = jnp.where(lane + first < count, 0.0, MASKED)
        absorb(keys, values, lambda: row)

    diagonal = lax.broadcasted_iota(jnp.int32, (tokens, tokens), 0) == lax.broadcasted_iota(
        jnp.int32, (tokens, tokens), 1
    )

    def positions_of(which):
        return positions_ref[pl.ds(which, 1), :]

    def as_column(row):
        spread = jnp.where(diagonal, jnp.broadcast_to(row, (tokens, tokens)), 0)
        return jnp.sum(spread.astype(F32), axis=1, keepdims=True)

    peer = (x * 2 + 1 - y_hi) * 2 + core
    mine = jnp.concatenate(
        [as_column(positions_of(ctx)), as_column(positions_of(peer))], axis=0
    )
    blocks = new_ref.shape[0] // tokens
    for b in range(blocks // 2):
        theirs = []
        for dc in range(2):
            source = (lax.rem(x + b, x_count) * 2 + y_hi) * 2 + lax.rem(core + dc, 2)
            theirs.append(positions_of(source).astype(F32))
        late = jnp.concatenate(theirs, axis=1) > mine
        bias_ref[...] = jnp.where(late, MASKED, 0.0)
        here = slice(2 * b * tokens, 2 * (b + 1) * tokens)
        absorb(new_ref[here, :W], new_ref[here, W:], lambda: bias_ref[...])

    lane = lax.broadcasted_iota(jnp.int32, (rows, W), 1)
    stats = jnp.zeros((rows, W), F32)
    for g in range(G):
        stats = jnp.where(lane == g, m_ref[g], stats)
        stats = jnp.where(lane == 8 + g, l_ref[g], stats)
    stats_ref[...] = stats


def attend(kept, slots, place, positions, queries, keys, values, new, x_count):
    rows = queries.shape[0]
    vmem = pl.BlockSpec(memory_space=pltpu.VMEM)
    smem = pl.BlockSpec(memory_space=pltpu.SMEM)
    work = rows * G * (keys.shape[0] // 2 + new.shape[0])
    return pl.pallas_call(
        functools.partial(attend_kernel, x_count),
        out_shape=[
            jax.ShapeDtypeStruct((G, rows, W), F32),
            jax.ShapeDtypeStruct((rows, W), F32),
        ],
        in_specs=[smem] * 3 + [vmem] * 5,
        out_specs=[vmem] * 2,
        scratch_shapes=[
            pltpu.VMEM((G, rows, W), F32),
            pltpu.VMEM((G, rows, W), F32),
            pltpu.VMEM((rows, rows), F32),
            pltpu.SMEM((kept.shape[1] + 8,), jnp.int32),
        ],
        compiler_params=pltpu.CompilerParams(vmem_limit_bytes=56 * 2**20),
        cost_estimate=pl.CostEstimate(
            flops=work * 4 * W, bytes_accessed=16 * 2**20, transcendentals=work
        ),
    )(kept, slots, place, positions, queries, keys, values, new)


def on_device(
    hidden,
    positions,
    w_query,
    key_matrix,
    value_matrix,
    w_out,
    stored_keys,
    stored_values,
    kept_pages,
    page_slot,
):
    tokens = hidden.shape[0]
    ctx_count, head_count = lax.axis_size("ctx"), lax.axis_size("head")
    x_count, z_count = ctx_count // 4, head_count // 2
    ctx, head = lax.axis_index("ctx"), lax.axis_index("head")
    table = positions.reshape(ctx_count, tokens)
    keys, values, new, queries, slab = gather(
        table, hidden, w_query, key_matrix, value_matrix, w_out, stored_keys, stored_values,
        x_count, z_count,
    )
    place = jnp.stack([ctx, head]).astype(jnp.int32)
    acc, stats = attend(
        kept_pages, page_slot, place, table, queries, keys.reshape(-1, W), values.reshape(-1, W),
        new.reshape(-1, 2 * W), x_count,
    )
    swap = [(i, i ^ 2) for i in range(ctx_count)]
    acc_in = lax.ppermute(acc[:, tokens:], "ctx", swap)
    stats_in = lax.ppermute(stats[tokens:], "ctx", swap)
    mine, theirs = stats[:tokens], stats_in
    heads = []
    for g in range(G):
        m1, m2 = mine[:, g : g + 1], theirs[:, g : g + 1]
        l1, l2 = mine[:, 8 + g : 9 + g], theirs[:, 8 + g : 9 + g]
        m = jnp.maximum(m1, m2)
        a1, a2 = jnp.exp(m1 - m), jnp.exp(m2 - m)
        total = l1 * a1 + l2 * a2
        heads.append((acc[g, :tokens] * (a1 / total) + acc_in[g] * (a2 / total)).astype(BF16))
    heads = jnp.concatenate(heads, axis=1)
    everyone = lax.all_gather(heads, "head", axis=1, tiled=True)
    return jnp.dot(everyone, slab.reshape(-1, slab.shape[2]), preferred_element_type=F32)


def solution(mesh):
    placed = (
        P("ctx", None),
        P(),
        P(None, "head"),
        P(None, "head"),
        P(None, "head"),
        P("head", None),
        P("ctx", "head"),
        P("ctx", "head"),
        P(),
        P(),
    )
    return jax.shard_map(
        on_device, mesh=mesh, in_specs=placed, out_specs=P("ctx", "head"), check_vma=False
    )
```

time: 594 us -> 214 us (0.36)
  waiting for transfers between devices: 327 us -> 78.7 us
  matrix products: 148 us -> 6.7 us
  Pallas kernels: 0 us -> 89.2 us
  starting transfers between devices: 56.3 us -> 5.81 us
  other arithmetic: 40.2 us -> 4.34 us
  local copies, waits for them, and re-layouts: 5.87 us -> 15.1 us
    dot_general x38 -> x1, matrix products: 148 us -> 6.7 us  [on_device(): jnp.dot(everyone, slab.reshape(-1, slab.shape[2]), preferred_element_type...]
    ppermute x64 -> x2, waiting for transfers between devices: 147 us -> 16.9 us  [the longest x1 16.9 us: on_device(): stats_in = lax.ppermute(stats[tokens:], 'ctx', swap)]
    reduce_scatter x1 -> x0, waiting for transfers between devices: 110 us -> none  [on_device(): lax.psum_scatter(partial_out, 'head', scatter_dimension=1, tiled=True)]
    pallas_call x0 -> x2, Pallas kernels: none -> 89.2 us  [the longest x1 49.8 us: gather(): pl.pallas_call(functools.partial(gather_kernel, x_count, z_count, float(r...]
    ppermute x64 -> x2, starting transfers between devices: 56.2 us -> 5.81 us  [the longest x1 5.49 us: on_device(): acc_in = lax.ppermute(acc[:, tokens:], 'ctx', swap)]
    reduce_sum x17 -> x0, other arithmetic: 36.4 us -> none  [absorb(): totals = totals * rescale + jnp.sum(weights, axis=-1)]
    unnamed x10 -> x26, local copies, waits for them, and re-layouts: 4.13 us -> 12.3 us
    all_gather x2 -> x1, waiting for transfers between devices: 69.6 us -> 61.8 us  [on_device(): everyone = lax.all_gather(heads, 'head', axis=1, tiled=True)]
  transfers between devices with their start and end apart: 67 -> 3, of which waited for: 19 -> 2; matrix products, arithmetic and copies ran while one was open for 28% -> 2% of each run, Pallas kernels for 0% -> 0%
where the time goes in v1:
time: 214 us; the launch traced here: 213 us
  Pallas kernels  89.2 us (42%)
  waiting for transfers between devices  78.7 us (37%)
  local copies, waits for them, and re-layouts  15.1 us (7%)
  between operations  13.5 us (6%)
  matrix products  6.7 us (3%)
  starting transfers between devices  5.81 us (3%)
  other arithmetic  4.34 us (2%)
    all_gather x1, waiting for transfers between devices, on_device(): everyone = lax.all_gather(heads, 'head', axis=1, tiled=True)  61.8 us
    pallas_call x1, Pallas kernels, gather(): pl.pallas_call(functools.partial(gather_kernel, x_count, z_count, float(r...  49.8 us
    pallas_call x1, Pallas kernels, attend(): pl.pallas_call(functools.partial(attend_kernel, x_count), out_shape=[jax....  39.4 us
    ppermute x1, waiting for transfers between devices, on_device(): stats_in = lax.ppermute(stats[tokens:], 'ctx', swap)  16.9 us
    unnamed x26, local copies, waits for them, and re-layouts  12.3 us
    dot_general x1, matrix products, on_device(): jnp.dot(everyone, slab.reshape(-1, slab.shape[2]), preferred_element_type...  6.7 us
    ppermute x1, starting transfers between devices, on_device(): acc_in = lax.ppermute(acc[:, tokens:], 'ctx', swap)  5.49 us
  transfers between devices with their start and end apart: 3, of which 2 were waited for; matrix products, arithmetic and copies ran while one was open for 2% of the time, Pallas kernels for 0%

profile of v1, /device:TPU:0, one launch (start us, length us, event | category | flops | bytes accessed | tf_op | source)
XLA Modules:
  0.0 213.4 jit_solution(15564508935141462901)
XLA Ops:
  6.5 0.7 reshape.15.positions_ref
  7.3 0.6 pad_add_fusion.place_ref
  7.9 1.7 copy-done
  9.6 1.3 copy-done.1
  10.9 1.3 copy-done.2
  12.2 1.0 copy-done.3
  13.2 1.0 copy-done.4
  14.2 49.8 %shard_map.100 = (bf16[8,1536,128]{2,1,0:T(8,128)(2,1)S(1)}, bf16[8,1536,128]{2,1,0:T(8,128)(2,1)S(1)}, bf16[8,256,256]{2,1,0:T(8,128)(2,1)S(1)}, bf16[512,640]{1,0:T(8,128)(2,1)S(1)}, bf16[8,640,640]{2,1,0:T(8,128)(2,1)}) custom-call(s32[16,256]{1,0:T(8,128)S(1)} %reshape.15.positions_ref, bf16[256,5120]{1,0:T(8,128)(2,1)S(1)} %copy-done, ...), custom_call_target="tpu_custom_call" | custom-call | tf_op jit(solution)/shard_map/pallas_call | solution.py:220
  64.1 1.7 copy-done.6
  65.8 1.6 copy-done.7
  67.5 1.0 copy-done.8
  68.4 0.8 copy-done.9
  69.3 39.4 %shard_map.101 = (f32[5,512,128]{2,1,0:T(8,128)}, f32[512,128]{1,0:T(8,128)}) custom-call(s32[8,96]{1,0:T(8,128)} %kept_ref.1, s32[192]{0:T(256)} %slot_ref.1, s32[2]{0:T(128)} %pad_add_fusion.place_ref, s32[16,256]{1,0:T(8,128)} %copy-done.5, bf16[512,640]{1,0:T(8,128)(2,1)} %copy-done.9, bf16[12288,128]{1,0:T(8,128)(2,1)} %bitcast.88, ...), custom_call_target="tpu_custom_call" | custom-call | flops 10737418240 | bytes 16777216 | tf_op jit(solution)/shard_map/pallas_call | solution.py:369
  108.6 1.2 slice.113
  109.9 5.5 %collective-permute-start.1 = (f32[5,256,128]{2,1,0:T(8,128)S(1)}, f32[5,256,128]{2,1,0:T(8,128)S(1)}, u32[]{:S(2)}, u32[]{:S(2)}) collective-permute-start(f32[5,256,128]{2,1,0:T(8,128)S(1)} %slice.113), channel_id=1, source_target_pairs={{0,16},{8,24},{16,0},{24,8},{32,48},{40,56},{48,32},{56,40},{64,80... | collective-permute-start | bytes 1966088 | tf_op jit(solution)/shard_map/ppermute | solution.py:417
  115.4 0.9 slice.109
  116.3 0.3 collective-permute-start
  116.6 16.9 %collective-permute-done = f32[256,128]{1,0:T(8,128)S(1)} collective-permute-done((f32[256,128]{1,0:T(8,128)S(1)}, f32[256,128]{1,0:T(8,128)S(1)}, u32[]{:S(2)}, u32[]{:S(2)}) %collective-permute-start) | collective-permute-done | bytes 131104 | tf_op jit(solution)/shard_map/ppermute | solution.py:418
  133.5 2.1 divide_reduce_fusion.1
  135.6 0.8 divide_reduce_fusion
  136.9 0.2 fusion.33
  137.3 0.7 copy-done.12
  138.0 61.8 %all-gather.2.cloned.1.call-done = bf16[256,5120]{1,0:T(8,128)(2,1)} async-done(((bf16[256,640]{1,0:T(8,128)(2,1)}), bf16[256,5120]{1,0:T(8,128)(2,1)}) %all-gather.2.cloned.1.call-update) | async-done | bytes 2621456 | tf_op jit(solution)/shard_map/all_gather | solution.py:429
  199.8 6.7 %fusion.35 = f32[256,640]{1,0:T(8,128)} fusion(bf16[256,5120]{1,0:T(8,128)(2,1)} %all-gather.2.cloned.1.call-done, bf16[5120,640]{1,0:T(8,128)(2,1)} %bitcast.91), kind=kOutput, calls=%fused_computation.71 | convolution fusion | flops 1677721600 | bytes 9830400 | tf_op jit(solution)/shard_map/dot_general | solution.py:430
  (23 shorter events, 0.7 us)
Async XLA Ops:
  6.5 193.3 %all-gather.2.cloned.1.call-start = ((), (), s32[]{:S(2)}) async-start(), calls=%async_computation | async-start | bytes 2949120 | tf_op jit(solution)/shard_map/all_gather | solution.py:429
  7.3 56.8 %copy-start.5 = (s32[16,256]{1,0:T(8,128)}, s32[16,256]{1,0:T(8,128)S(1)}, u32[]{:S(2)}) copy-start(s32[16,256]{1,0:T(8,128)S(1)} %reshape.15.positions_ref) | copy-start | bytes 49156
  7.9 1.7 copy-start
  9.6 1.3 copy-start.1
  10.9 1.3 copy-start.2
  12.2 1.0 copy-start.3
  13.2 1.0 copy-start.4
  64.1 1.7 copy-start.6
  65.8 1.6 copy-start.7
  67.4 1.0 copy-start.8
  68.4 0.8 copy-start.9
  108.6 27.0 %copy-start.10 = (f32[512,128]{1,0:T(8,128)S(1)}, f32[512,128]{1,0:T(8,128)}, u32[]{:S(2)}) copy-start(f32[512,128]{1,0:T(8,128)} %get-tuple-element.17) | copy-start | bytes 786436
  108.6 27.8 %copy-start.11 = (f32[5,512,128]{2,1,0:T(8,128)S(1)}, f32[5,512,128]{2,1,0:T(8,128)}, u32[]{:S(2)}) copy-start(f32[5,512,128]{2,1,0:T(8,128)} %get-tuple-element.16) | copy-start | bytes 3932164
  109.9 26.6 %collective-permute-start.1 = (f32[5,256,128]{2,1,0:T(8,128)S(1)}, f32[5,256,128]{2,1,0:T(8,128)S(1)}, u32[]{:S(2)}, u32[]{:S(2)}) collective-permute-start(f32[5,256,128]{2,1,0:T(8,128)S(1)} %slice.113), channel_id=1, source_target_pairs={{0,16},{8,24},{16,0},{24,8},{32,48},{40,56},{48,32},{56,40},{64,80... | collective-permute-start | bytes 1966088 | tf_op jit(solution)/shard_map/ppermute | solution.py:417
  116.3 17.2 %collective-permute-start = (f32[256,128]{1,0:T(8,128)S(1)}, f32[256,128]{1,0:T(8,128)S(1)}, u32[]{:S(2)}, u32[]{:S(2)}) collective-permute-start(f32[256,128]{1,0:T(8,128)S(1)} %slice.109), channel_id=1, source_target_pairs={{0,16},{8,24},{16,0},{24,8},{32,48},{40,56},{48,32},{56,40},{64,80... | collective-permute-start | bytes 393224 | tf_op jit(solution)/shard_map/ppermute | solution.py:418
  137.3 0.7 copy-start.12
Sparse Core Ops, SparseCore 0:
  138.1 61.6 all-gather.1

commit v2 on v1

--- a/solution.py
+++ b/solution.py
@@ -242,7 +242,7 @@
             pltpu.SemaphoreType.DMA((5,)),
         ],
         compiler_params=pltpu.CompilerParams(
-            collective_id=0, has_side_effects=True, vmem_limit_bytes=40 * 2**20
+            collective_id=0, has_side_effects=True, vmem_limit_bytes=60 * 2**20
         ),
     )(positions, hidden, w_query, w_key, w_value, w_out, keys, values)
 
@@ -289,7 +289,6 @@
 
     def absorb(keys, values, bias):
         width = keys.shape[0] // W
-        values = jnp.concatenate([values, jnp.ones_like(values)], axis=1)
         for g in range(G):
             q = q_ref[:, g * W : (g + 1) * W]
             s = lax.dot_general(q, keys, (((1,), (1,)), ((), ())), preferred_element_type=F32)
@@ -298,31 +297,36 @@
             m_old = m_ref[g]
             m_new = jnp.maximum(m_old, jnp.max(s, axis=1, keepdims=True))
             rescale = jnp.exp(m_old - m_new)
-            p = jnp.exp(s - jnp.concatenate([m_new] * width, axis=1)).astype(BF16)
-            summed = jnp.dot(p, values, preferred_element_type=F32)
-            l_ref[g] = l_ref[g] * rescale + summed[:, W:]
-            acc_ref[g] = acc_ref[g] * rescale + summed[:, :W]
+            p = jnp.exp(s - jnp.concatenate([m_new] * width, axis=1))
+            sums = sum(p[:, c * W : (c + 1) * W] for c in range(width))
+            l_ref[g] = l_ref[g] * rescale + sums
+            acc_ref[g] = acc_ref[g] * rescale + jnp.dot(
+                p.astype(BF16), values, preferred_element_type=F32
+            )
             m_ref[g] = m_new
 
-    def pages(first):
+    def pages(first, many):
         ks, vs = [], []
-        for j in range(step):
+        for j in range(many):
             here = pl.ds(pl.multiple_of(list_ref[first + j] * PAGE, PAGE), PAGE)
             ks.append(k_ref[here, :])
             vs.append(v_ref[here, :])
         return jnp.concatenate(ks, axis=0), jnp.concatenate(vs, axis=0)
 
     def full(i, _):
-        keys, values = pages(i * step)
-        absorb(keys, values, None)
+        absorb(*pages(i * 2 * step, 2 * step), None)
         return 0
 
-    lax.fori_loop(0, count // step, full, 0)
+    lax.fori_loop(0, count // (2 * step), full, 0)
+
+    @pl.when(count % (2 * step) >= step)
+    def _():
+        absorb(*pages(count // (2 * step) * (2 * step), step), None)
 
     @pl.when(count % step > 0)
     def _():
         first = count // step * step
-        keys, values = pages(first)
+        keys, values = pages(first, step)
         lane = lax.broadcasted_iota(jnp.int32, (1, step * PAGE), 1) // PAGE
         row = jnp.where(lane + first < count, 0.0, MASKED)
         absorb(keys, values, lambda: row)
@@ -357,7 +361,7 @@
     stats = jnp.zeros((rows, W), F32)
     for g in range(G):
         stats = jnp.where(lane == g, m_ref[g], stats)
-        stats = jnp.where(lane == 8 + g, l_ref[g], stats)
+        stats = jnp.where(lane == 8 + g, jnp.sum(l_ref[g], axis=1, keepdims=True), stats)
     stats_ref[...] = stats
 
 
@@ -380,11 +384,172 @@
             pltpu.VMEM((rows, rows), F32),
             pltpu.SMEM((kept.shape[1] + 8,), jnp.int32),
         ],
-        compiler_params=pltpu.CompilerParams(vmem_limit_bytes=56 * 2**20),
+        compiler_params=pltpu.CompilerParams(vmem_limit_bytes=60 * 2**20),
         cost_estimate=pl.CostEstimate(
             flops=work * 4 * W, bytes_accessed=16 * 2**20, transcendentals=work
         ),
     )(kept, slots, place, positions, queries, keys, values, new)
+
+
+def finish_kernel(
+    x_count,
+    z_count,
+    acc_ref,
+    stats_ref,
+    slab_ref,
+    out_ref,
+    acc_own,
+    acc_in,
+    stats_own,
+    stats_in,
+    slab_vmem,
+    heads,
+    send_sem,
+    recv_sem,
+    load_sem,
+):
+    ctx, head, core, at = places(x_count)
+    z, y_lo = head // 2, head % 2
+    tokens = stats_own.shape[0]
+    y_peer = at(dy=1)
+
+    def head_at(dz, dl):
+        return lax.rem(z + dz, z_count) * 2 + lax.rem(y_lo + dl, 2)
+
+    above, below, beside = head_at(1, 0), head_at(z_count - 1, 0), head_at(0, 1)
+    barrier = pltpu.get_barrier_semaphore()
+    met = [(y_peer, head), (ctx, above), (ctx, below), (ctx, beside)]
+    for device in met:
+        pl.semaphore_signal(barrier, inc=1, device_id=device, device_id_type=MESH)
+    pl.semaphore_wait(barrier, len(met))
+
+    counter = [0]
+    started = []
+
+    def send(source, target, device):
+        i = counter[0]
+        counter[0] += 1
+        copy = pltpu.make_async_remote_copy(
+            src_ref=source,
+            dst_ref=target,
+            send_sem=send_sem.at[i],
+            recv_sem=recv_sem.at[i],
+            device_id=device,
+            device_id_type=MESH,
+        )
+        copy.start()
+        started.append(copy)
+        return copy
+
+    rows_own, rows_peer = pl.ds(0, tokens), pl.ds(tokens, tokens)
+    stats_copy = send(stats_ref.at[rows_peer], stats_in, (y_peer, head))
+    parts = [send(acc_ref.at[g, rows_peer], acc_in.at[g], (y_peer, head)) for g in range(G)]
+    loads = [
+        pltpu.make_async_copy(stats_ref.at[rows_own], stats_own, load_sem.at[0]),
+        pltpu.make_async_copy(acc_ref.at[:, rows_own], acc_own, load_sem.at[1]),
+        pltpu.make_async_copy(slab_ref, slab_vmem, load_sem.at[2]),
+    ]
+    for load in loads:
+        load.start()
+    loads[0].wait()
+    loads[1].wait()
+    stats_copy.wait_recv()
+    m1, m2 = stats_own[:, 0:8], stats_in[:, 0:8]
+    l1, l2 = stats_own[:, 8:16], stats_in[:, 8:16]
+    m = jnp.maximum(m1, m2)
+    a1, a2 = jnp.exp(m1 - m), jnp.exp(m2 - m)
+    total = l1 * a1 + l2 * a2
+
+    def pass_on(who, g, device):
+        return send(heads.at[who, g], heads.at[who, g], (ctx, device))
+
+    first = [True]
+
+    def use_first(who, g):
+        if first[0]:
+            loads[2].wait()
+        use_now(who, g)
+
+    def use_now(who, g):
+        product = jnp.dot(
+            heads[who, g], slab_vmem[who, g * W : (g + 1) * W, :], preferred_element_type=F32
+        )
+        if first[0]:
+            out_ref[...] = product
+            first[0] = False
+        else:
+            out_ref[...] += product
+
+    up, down, side, up_side, down_side, two, two_side = ({} for _ in range(7))
+    for t in range(G + 3):
+        g = t
+        if g < G:
+            parts[g].wait_recv()
+            weight1 = a1[:, g : g + 1] / total[:, g : g + 1]
+            weight2 = a2[:, g : g + 1] / total[:, g : g + 1]
+            heads[head, g] = (acc_own[g] * weight1 + acc_in[g] * weight2).astype(BF16)
+            side[g] = pass_on(head, g, beside)
+            up[g] = pass_on(head, g, above)
+            down[g] = pass_on(head, g, below)
+            use_first(head, g)
+        g = t - 1
+        if 0 <= g < G:
+            side[g].wait_recv()
+            up_side[g] = pass_on(beside, g, above)
+            down_side[g] = pass_on(beside, g, below)
+            up[g].wait_recv()
+            down[g].wait_recv()
+            if g % 2 == 0:
+                two[g] = pass_on(below, g, above)
+            else:
+                two[g] = pass_on(above, g, below)
+            use_now(beside, g)
+            use_now(below, g)
+            use_now(above, g)
+        g = t - 2
+        if 0 <= g < G:
+            up_side[g].wait_recv()
+            down_side[g].wait_recv()
+            if g % 2 == 1:
+                two_side[g] = pass_on(head_at(z_count - 1, 1), g, above)
+            else:
+                two_side[g] = pass_on(head_at(1, 1), g, below)
+            use_now(head_at(z_count - 1, 1), g)
+            use_now(head_at(1, 1), g)
+        g = t - 3
+        if 0 <= g < G:
+            two[g].wait_recv()
+            use_now(head_at(2, 0), g)
+            two_side[g].wait_recv()
+            use_now(head_at(2, 1), g)
+    for copy in started:
+        copy.wait_send()
+
+
+def finish(acc, stats, slab, x_count, z_count):
+    tokens = stats.shape[0] // 2
+    anywhere = pl.BlockSpec(memory_space=pl.ANY)
+    copies = 1 + G * 8
+    return pl.pallas_call(
+        functools.partial(finish_kernel, x_count, z_count),
+        out_shape=jax.ShapeDtypeStruct((tokens, slab.shape[2]), F32),
+        in_specs=[anywhere] * 3,
+        out_specs=pl.BlockSpec(memory_space=pltpu.VMEM),
+        scratch_shapes=[
+            pltpu.VMEM((G, tokens, W), F32),
+            pltpu.VMEM((G, tokens, W), F32),
+            pltpu.VMEM((tokens, W), F32),
+            pltpu.VMEM((tokens, W), F32),
+            pltpu.VMEM(slab.shape, BF16),
+            pltpu.VMEM((2 * z_count, G, tokens, W), BF16),
+            pltpu.SemaphoreType.DMA((copies,)),
+            pltpu.SemaphoreType.DMA((copies,)),
+            pltpu.SemaphoreType.DMA((3,)),
+        ],
+        compiler_params=pltpu.CompilerParams(
+            collective_id=1, has_side_effects=True, vmem_limit_bytes=60 * 2**20
+        ),
+    )(acc, stats, slab)
 
 
 def on_device(
@@ -413,21 +578,7 @@
         kept_pages, page_slot, place, table, queries, keys.reshape(-1, W), values.reshape(-1, W),
         new.reshape(-1, 2 * W), x_count,
     )
-    swap = [(i, i ^ 2) for i in range(ctx_count)]
-    acc_in = lax.ppermute(acc[:, tokens:], "ctx", swap)
-    stats_in = lax.ppermute(stats[tokens:], "ctx", swap)
-    mine, theirs = stats[:tokens], stats_in
-    heads = []
-    for g in range(G):
-        m1, m2 = mine[:, g : g + 1], theirs[:, g : g + 1]
-        l1, l2 = mine[:, 8 + g : 9 + g], theirs[:, 8 + g : 9 + g]
-        m = jnp.maximum(m1, m2)
-        a1, a2 = jnp.exp(m1 - m), jnp.exp(m2 - m)
-        total = l1 * a1 + l2 * a2
-        heads.append((acc[g, :tokens] * (a1 / total) + acc_in[g] * (a2 / total)).astype(BF16))
-    heads = jnp.concatenate(heads, axis=1)
-    everyone = lax.all_gather(heads, "head", axis=1, tiled=True)
-    return jnp.dot(everyone, slab.reshape(-1, slab.shape[2]), preferred_element_type=F32)
+    return finish(acc, stats, slab, x_count, z_count)
 
 
 def solution(mesh):

time: 214 us -> 156 us (0.73)
  waiting for transfers between devices: 78.7 us -> 0 us
  Pallas kernels: 89.2 us -> 152 us
  between operations: 13.5 us -> 0.02 us
  local copies, waits for them, and re-layouts: 15.1 us -> 3.29 us
  matrix products: 6.7 us -> 0 us
  starting transfers between devices: 5.81 us -> 0 us
  other arithmetic: 4.34 us -> 0.56 us
    all_gather x1 -> x0, waiting for transfers between devices: 61.8 us -> none  [on_device(): everyone = lax.all_gather(heads, 'head', axis=1, tiled=True)]
    pallas_call x0 -> x1, Pallas kernels: none -> 48.6 us  [finish(): pl.pallas_call(functools.partial(finish_kernel, x_count, z_count), out_sh...]
    ppermute x2 -> x0, waiting for transfers between devices: 16.9 us -> none  [the longest x1 16.9 us: on_device(): stats_in = lax.ppermute(stats[tokens:], 'ctx', swap)]
    unnamed x26 -> x1, local copies, waits for them, and re-layouts: 12.3 us -> 1.97 us
    pallas_call x1, Pallas kernels: 39.4 us -> 46.3 us  [attend(): pl.pallas_call(functools.partial(attend_kernel, x_count), out_shape=[jax....]
    pallas_call x1, Pallas kernels: 49.8 us -> 56.6 us  [gather(): pl.pallas_call(functools.partial(gather_kernel, x_count, z_count, float(r...]
    dot_general x1 -> x0, matrix products: 6.7 us -> none  [on_device(): jnp.dot(everyone, slab.reshape(-1, slab.shape[2]), preferred_element_type...]
    ppermute x2 -> x0, starting transfers between devices: 5.81 us -> none  [the longest x1 5.49 us: on_device(): acc_in = lax.ppermute(acc[:, tokens:], 'ctx', swap)]
  transfers between devices with their start and end apart: 3 -> 0, of which waited for: 2 -> 0; matrix products, arithmetic and copies ran while one was open for 2% -> 0% of each run, Pallas kernels for 0% -> 0%
where the time goes in v2:
time: 156 us; the launch traced here: 155 us
  Pallas kernels  152 us (97%)
  local copies, waits for them, and re-layouts  3.29 us (2%)
    pallas_call x1, Pallas kernels, gather(): pl.pallas_call(functools.partial(gather_kernel, x_count, z_count, float(r...  56.6 us
    pallas_call x1, Pallas kernels, finish(): pl.pallas_call(functools.partial(finish_kernel, x_count, z_count), out_sh...  48.6 us
    pallas_call x1, Pallas kernels, attend(): pl.pallas_call(functools.partial(attend_kernel, x_count), out_shape=[jax....  46.3 us

profile of v2, /device:TPU:0, one launch (start us, length us, event | category | flops | bytes accessed | tf_op | source)
XLA Modules:
  0.0 155.4 jit_solution(5614415372354273653)
XLA Ops:
  0.0 0.6 pad_add_fusion.place_ref
  0.6 1.3 reshape.12.positions_ref
  1.9 56.6 %shard_map.100 = (bf16[8,1536,128]{2,1,0:T(8,128)(2,1)}, bf16[8,1536,128]{2,1,0:T(8,128)(2,1)}, bf16[8,256,256]{2,1,0:T(8,128)(2,1)}, bf16[512,640]{1,0:T(8,128)(2,1)}, bf16[8,640,640]{2,1,0:T(8,128)(2,1)}) custom-call(s32[16,256]{1,0:T(8,128)} %reshape.12.positions_ref, bf16[256,5120]{1,0:T(8,128)(2,1)} %hidden_ref.1, bf16[5120,640]{1,0:T(8,128)(2,1)} %w_query_ref.1, ...), custom_call_target="tpu_custom_call" | custom-call | tf_op jit(solution)/shard_map/pallas_call | solution.py:220
  58.5 46.3 %shard_map.101 = (f32[5,512,128]{2,1,0:T(8,128)}, f32[512,128]{1,0:T(8,128)}) custom-call(s32[8,96]{1,0:T(8,128)} %kept_ref.1, s32[192]{0:T(256)} %slot_ref.1, s32[2]{0:T(128)} %pad_add_fusion.place_ref, s32[16,256]{1,0:T(8,128)} %reshape.12.positions_ref, bf16[512,640]{1,0:T(8,128)(2,1)} %get-tuple-element.12.q_ref, bf16[12288,128]{1,0:T(8,128)(2,1)} %bitcast.5, ...), custom_call_target="tpu_custom_call" | custom-call | flops 10737418240 | bytes 16777216 | tf_op jit(solution)/shard_map/pallas_call | solution.py:373
  104.8 48.6 %shard_map.102 = f32[256,640]{1,0:T(8,128)} custom-call(f32[5,512,128]{2,1,0:T(8,128)} %get-tuple-element.16.acc_ref, f32[512,128]{1,0:T(8,128)} %get-tuple-element.17.stats_ref, bf16[8,640,640]{2,1,0:T(8,128)(2,1)} %get-tuple-element.18.slab_ref), custom_call_target="tpu_custom_call" | custom-call | tf_op jit(solution)/shard_map/pallas_call | solution.py:533
  153.4 2.0 %copy.12 = f32[256,640]{1,0:T(8,128)} copy(f32[256,640]{1,0:T(8,128)} %shard_map.102) | data formatting | bytes 1310720
